TPU v7x, 32 devices: a whole 2x2x4 slice. The times are simulated.
32 devices in a mesh: aux: 4 (over y, core), row: 8 (over z, x).
Axes of the slice: x: 2, y: 2, z: 4, core: 2. Of those that a mesh axis runs over, the one named last changes fastest.
Arguments:
- integrals: bfloat16 [16, 16, 4, 256, 256], P('aux', 'row'), may hold values from -6 to 6
- block_columns: int32 [16, 4], P('row'), may hold values from 0 to 15, as said below
- orbitals: bfloat16 [4096, 2048], P('row'), may hold values from -0.1875 to 0.1875
- occ_mask: int32 [16, 8], replicated, may hold values from 0 to 1, as said below
Outputs:
- exchange: float32 [4096, 1536], P('row', 'aux')
Inputs may be any that keep to these rules, and one draw needn't show every extreme that they name: `block_columns`: each row block has 4 different column blocks, each lying on the same row device as the row block or on the one beside it. `occ_mask`: entry (b, s) is 1 when row block b lies on row device s, and 0 when it lies on a device more than one away from s.
All inputs are finite; a program needn't handle non-finite values.
Results may differ from a plain program's by a relative error of at most 0.0018.
Values may be sent and summed in bfloat16 or wider, within the bound.
A program may use at most 128 MiB of HBM per device.

v0:
```python
import jax
import jax.numpy as jnp
from jax import lax
from jax.sharding import PartitionSpec as P


def passed_along(block, axis, distance):
    devices = range(lax.axis_size(axis))
    route = [(i - distance, i) for i in devices if i - distance in devices]
    return lax.ppermute(block, axis, route)


def padded_2(block, sides, width):
    for axis, dim in sides:
        count = lax.axis_size(axis)
        forward = [(i, i + 1) for i in range(count - 1)]
        backward = [(target, source) for source, target in forward]
        low = lax.ppermute(
            lax.slice_in_dim(block, block.shape[dim] - width, None, axis=dim), axis, forward
        )
        high = lax.ppermute(lax.slice_in_dim(block, 0, width, axis=dim), axis, backward)
        block = jnp.concatenate([low, block, high], axis=dim)
    return block


def send_slice(masked, position, slice_width, offset):
    outgoing = lax.dynamic_slice_in_dim(masked, (position + offset) * slice_width, slice_width, 1)
    return passed_along(outgoing, "row", offset)


def pass_rows(partial_value, offset):
    return passed_along(partial_value, "row", offset)


def reduce_aux(partial_value):
    return lax.psum_scatter(partial_value, "aux", scatter_dimension=1, tiled=True)


def on_device(integrals, block_columns, orbitals, occ_mask):
    aux_count, row_blocks, kept_blocks, block_size, _ = integrals.shape
    own_rows, occ_count = orbitals.shape
    row_devices = lax.axis_size("row")
    position = lax.axis_index("row")
    slice_width = occ_count // row_devices
    weight_scale = 1.0 / (aux_count * lax.axis_size("aux") * slice_width) ** 0.5
    extended = padded_2(orbitals, (("row", 0),), own_rows)
    ext_blocks = extended.reshape(3 * row_blocks, block_size, occ_count)
    local_columns = block_columns - (position - 1) * row_blocks
    gathered = ext_blocks[local_columns]
    product = jnp.einsum(
        "prkml,rklj->pjrm", integrals, gathered, preferred_element_type=jnp.float32
    )
    mask_rows = lax.dynamic_slice_in_dim(occ_mask, position * row_blocks, row_blocks, 0)
    factor = jnp.repeat(mask_rows.T.astype(jnp.float32), slice_width, axis=0)
    masked = (
        (product * factor[None, :, :, None])
        .astype(jnp.bfloat16)
        .reshape(aux_count, occ_count, own_rows)
    )
    own_slice = lax.dynamic_slice_in_dim(masked, position * slice_width, slice_width, 1)
    from_left = send_slice(masked, position, slice_width, 1)
    from_right = send_slice(masked, position, slice_width, -1)
    window = jnp.concatenate([from_left, own_slice, from_right], 2)
    exchange_slab = (
        jnp.einsum("pjm,pjn->mn", window, window, preferred_element_type=jnp.float32) * weight_scale
    )
    framed = []
    for place in range(3):
        strip = exchange_slab[place * own_rows : (place + 1) * own_rows]
        padded = jnp.pad(strip, ((0, 0), (own_rows, own_rows)))
        framed.append(padded[:, place * own_rows : place * own_rows + 3 * own_rows])
    frames = jnp.stack(framed, 0)
    partial_value = frames[1] + pass_rows(frames[0], -1) + pass_rows(frames[2], 1)
    reduced = reduce_aux(partial_value)
    return reduced


def solution(mesh):
    in_specs = (P("aux", "row", None, None, None), P("row", None), P("row", None), P())
    out_specs = P("row", "aux")
    return jax.shard_map(
        on_device, mesh=mesh, in_specs=in_specs, out_specs=out_specs, check_vma=False
    )
```

profile of v0, /device:TPU:13, one launch (start us, length us, event | category | flops | bytes accessed | tf_op | source)
XLA Modules:
  0.0 386.1 jit_solution(17910137094055751445)
XLA Ops:
  6.5 3.1 collective-permute-start
  9.7 3.1 collective-permute-start.1
  12.7 0.7 compare_select_fusion
  13.4 0.1 reshape.11
  13.5 0.8 convert_bitcast_fusion
  14.3 0.1 copy.9
  14.4 0.1 broadcast_bitcast_fusion
  14.5 84.7 %collective-permute-done = bf16[512,2048]{1,0:T(8,128)(2,1)S(1)} collective-permute-done((bf16[512,2048]{1,0:T(8,128)(2,1)}, bf16[512,2048]{1,0:T(8,128)(2,1)S(1)}, u32[]{:S(2)}, u32[]{:S(2)}) %collective-permute-start) | collective-permute-done | bytes 2097184 | tf_op jit(solution)/shard_map/ppermute | solution.py:18
  99.2 2.9 collective-permute-done.1
  102.1 5.4 %pad_maximum_fusion = bf16[1536,2048]{1,0:T(8,128)(2,1)} fusion(bf16[512,2048]{1,0:T(8,128)(2,1)} %collective-permute-done.1, bf16[512,2048]{1,0:T(8,128)(2,1)} %param.6, bf16[512,2048]{1,0:T(8,128)(2,1)S(1)} %collective-permute-done), kind=kLoop, calls=%fused_computation.4 | loop fusion | flops 18874368 | bytes 12582912 | tf_op jit(solution)/shard_map/concatenate | solution.py:22
  107.6 7.5 %gather_fusion = bf16[8,256,2048]{2,1,0:T(8,128)(2,1)} fusion(bf16[6,256,2048]{2,1,0:T(8,128)(2,1)} %bitcast.24, s32[1024]{0:T(1024)S(1)} %pad_clamp_fusion), kind=kCustom, calls=%fused_computation | custom fusion | bytes 16777248 | tf_op jit(solution)/shard_map/gather | solution.py:49
  115.0 14.5 %fusion = bf16[4,2048,2,256]{1,3,0,2:T(8,128)(2,1)} fusion(f32[2048,2]{0,1:T(2,128)S(1)} %bitcast.27, bf16[2,4,256,2048,1]{3,2,1,4,0:T(8,128)(2,1)} %bitcast.26, bf16[4,2,4,256,256]{4,3,2,1,0:T(8,128)(2,1)} %param.4), kind=kOutput, calls=%fused_computation.2 | convolution fusion | flops 8598323200 | bytes 20987904 | tf_op jit(solution)/shard_map/prkml,rklj->pjrm/dot_general | solution.py:50
  129.6 8.3 %copy.10 = bf16[4,2048,2,256]{1,3,2,0:T(8,128)(2,1)} copy(bf16[4,2048,2,256]{1,3,0,2:T(8,128)(2,1)} %fusion) | data formatting | bytes 16777216 | tf_op jit(solution)/shard_map/convert_element_type | solution.py:57
  137.8 2.1 constant_dynamic-slice_fusion.2
  139.9 1.3 copy.18
  141.3 0.5 copy.20
  141.8 1.9 collective-permute-start.3
  143.7 3.5 collective-permute-start.2
  147.3 0.5 copy.19
  147.8 42.7 %collective-permute-done.3 = bf16[4,256,512]{2,1,0:T(8,128)(2,1)} collective-permute-done((bf16[4,256,512]{2,1,0:T(8,128)(2,1)S(1)}, bf16[4,256,512]{2,1,0:T(8,128)(2,1)}, u32[]{:S(2)}, u32[]{:S(2)}) %collective-permute-start.3) | collective-permute-done | bytes 1048608 | tf_op jit(solution)/shard_map/ppermute | solution.py:10
  190.5 0.0 collective-permute-done.2
  190.5 7.4 %bitcast_multiply_fusion.1 = f32[1536,1536]{1,0:T(8,128)S(1)} fusion(bf16[4,256,512]{2,1,0:T(8,128)(2,1)} %collective-permute-done.3, bf16[4,256,512]{2,1,0:T(8,128)(2,1)S(1)} %copy.19, bf16[4,256,512]{2,1,0:T(8,128)(2,1)} %collective-permute-done.2), kind=kOutput, calls=%fused_computation.3 | convolution fusion | flops 4843634688 | bytes 12582912 | tf_op jit(solution)/shard_map/pjm,pjn->mn/dot_general | solution.py:65
  197.9 0.4 fusion.9
  198.4 0.4 pad_slice_fusion.1
  198.8 0.4 pad_slice_fusion
  199.2 3.5 collective-permute-start.5
  202.7 2.7 collective-permute-start.4
  205.4 131.7 %collective-permute-done.5 = f32[512,1536]{1,0:T(8,128)S(1)} collective-permute-done((f32[512,1536]{1,0:T(8,128)S(1)}, f32[512,1536]{1,0:T(8,128)S(1)}, u32[]{:S(2)}, u32[]{:S(2)}) %collective-permute-start.5) | collective-permute-done | bytes 3145760 | tf_op jit(solution)/shard_map/ppermute | solution.py:10
  337.1 2.4 collective-permute-done.4
  339.4 2.7 fusion.2
  342.1 0.0 reduce-scatter.2.cloned.1.call-update
  342.2 37.1 %reduce-scatter.2.cloned.1.call-done = f32[512,384]{1,0:T(8,128)} async-done(((f32[512,1536]{1,0:T(8,128)}), f32[512,384]{1,0:T(8,128)}) %reduce-scatter.2.cloned.1.call-update) | async-done | bytes 786448 | tf_op jit(solution)/shard_map/reduce_scatter | solution.py:36
  (3 shorter events, 0.0 us)
Async XLA Ops:
  6.5 372.7 %reduce-scatter.2.cloned.1.call-start = ((), (), s32[]{:S(2)}) async-start(), calls=%async_computation.1 | async-start | bytes 3932160 | tf_op jit(solution)/shard_map/reduce_scatter | solution.py:36
  6.5 92.7 %collective-permute-start = (bf16[512,2048]{1,0:T(8,128)(2,1)}, bf16[512,2048]{1,0:T(8,128)(2,1)S(1)}, u32[]{:S(2)}, u32[]{:S(2)}) collective-permute-start(bf16[512,2048]{1,0:T(8,128)(2,1)} %param.6), channel_id=1, source_target_pairs={{0,1},{1,2},{2,3},{3,4},{4,5},{5,6},{6,7},{8,9},{9,10},{10,11},{11... | collective-permute-start | bytes 6291464 | tf_op jit(solution)/shard_map/ppermute | solution.py:18
  9.7 92.5 %collective-permute-start.1 = (bf16[512,2048]{1,0:T(8,128)(2,1)}, bf16[512,2048]{1,0:T(8,128)(2,1)}, u32[]{:S(2)}, u32[]{:S(2)}) collective-permute-start(bf16[512,2048]{1,0:T(8,128)(2,1)} %param.6), channel_id=1, source_target_pairs={{1,0},{2,1},{3,2},{4,3},{5,4},{6,5},{7,6},{9,8},{10,9},{11,10},{12... | collective-permute-start | bytes 6291464 | tf_op jit(solution)/shard_map/ppermute | solution.py:21
  141.8 48.7 %collective-permute-start.3 = (bf16[4,256,512]{2,1,0:T(8,128)(2,1)S(1)}, bf16[4,256,512]{2,1,0:T(8,128)(2,1)}, u32[]{:S(2)}, u32[]{:S(2)}) collective-permute-start(bf16[4,256,512]{2,1,0:T(8,128)(2,1)S(1)} %copy.20), channel_id=1, source_target_pairs={{1,0},{2,1},{3,2},{4,3},{5,4},{6,5},{7,6},{9,8},{10,9},{11,10},{12... | collective-permute-start | bytes 3145736 | tf_op jit(solution)/shard_map/ppermute | solution.py:10
  143.7 46.8 %collective-permute-start.2 = (bf16[4,256,512]{2,1,0:T(8,128)(2,1)}, bf16[4,256,512]{2,1,0:T(8,128)(2,1)}, u32[]{:S(2)}, u32[]{:S(2)}) collective-permute-start(bf16[4,256,512]{2,1,0:T(8,128)(2,1)} %copy.18), channel_id=1, source_target_pairs={{0,1},{1,2},{2,3},{3,4},{4,5},{5,6},{6,7},{8,9},{9,10},{10,11},{11... | collective-permute-start | bytes 3145736 | tf_op jit(solution)/shard_map/ppermute | solution.py:10
  199.2 137.9 %collective-permute-start.5 = (f32[512,1536]{1,0:T(8,128)S(1)}, f32[512,1536]{1,0:T(8,128)S(1)}, u32[]{:S(2)}, u32[]{:S(2)}) collective-permute-start(f32[512,1536]{1,0:T(8,128)S(1)} %pad_slice_fusion), channel_id=1, source_target_pairs={{0,1},{1,2},{2,3},{3,4},{4,5},{5,6},{6,7},{8,9},{9,10},{10,11},{11... | collective-permute-start | bytes 9437192 | tf_op jit(solution)/shard_map/ppermute | solution.py:10
  202.7 136.7 %collective-permute-start.4 = (f32[512,1536]{1,0:T(8,128)S(1)}, f32[512,1536]{1,0:T(8,128)S(1)}, u32[]{:S(2)}, u32[]{:S(2)}) collective-permute-start(f32[512,1536]{1,0:T(8,128)S(1)} %pad_slice_fusion.1), channel_id=1, source_target_pairs={{1,0},{2,1},{3,2},{4,3},{5,4},{6,5},{7,6},{9,8},{10,9},{11,10},{12... | collective-permute-start | bytes 9437192 | tf_op jit(solution)/shard_map/ppermute | solution.py:10
Sparse Core Ops, SparseCore 0:
  342.3 36.8 reduce-scatter.1
where the time goes:
time: 389 us; the launch traced here: 386 us
  waiting for transfers between devices  301 us (77%)
  matrix products  21.9 us (6%)
  local copies, waits for them, and re-layouts  21.7 us (6%)
  starting transfers between devices  17.8 us (5%)
  between operations  13.5 us (3%)
  other arithmetic  9.58 us (2%)
    ppermute x4, waiting for transfers between devices, passed_along(): return lax.ppermute(block, axis, route)  177 us
    ppermute x1, waiting for transfers between devices, padded_2(): lax.ppermute(lax.slice_in_dim(block, block.shape[dim] - width, None, axis...  84.7 us
    reduce_scatter x1, waiting for transfers between devices, reduce_aux(): lax.psum_scatter(partial_value, 'aux', scatter_dimension=1, tiled=True)  37.1 us
    dot_general x1, matrix products, on_device(): jnp.einsum('prkml,rklj->pjrm', integrals, gathered, preferred_element_typ...  14.5 us
    ppermute x4, starting transfers between devices, passed_along(): return lax.ppermute(block, axis, route)  11.6 us
    convert_element_type x1, local copies, waits for them, and re-layouts, on_device(): masked = (product * factor[None, :, :, None]).astype(jnp.bfloat16).reshap...  8.28 us
  transfers between devices with their start and end apart: 7, of which 6 were waited for; matrix products, arithmetic and copies ran while one was open for 1% of the time, Pallas kernels for 0%

commit v1 on v0

v1 whole, which is shorter than its diff:
```python
import functools

import jax
import jax.numpy as jnp
from jax import lax
from jax.experimental import pallas as pl
from jax.experimental.pallas import tpu as pltpu
from jax.sharding import PartitionSpec as P

MESH = pl.DeviceIdType.MESH
NT = (((1,), (1,)), ((), ()))


def overlap(lo, hi, start, stop):
    lo, hi = max(lo, start), min(hi, stop)
    return (lo, hi) if lo < hi else None


def kernel(
    aux,
    rows,
    scale,
    cols_ref,
    mask_ref,
    orb_ref,
    int_hbm,
    out_ref,
    ints,
    e0,
    e1,
    e2,
    h0,
    h1,
    h2,
    rh0,
    rh1,
    d_buf,
    w_buf,
    v_buf,
    s_rec,
    v_rec,
    int_sem,
    orb_send,
    orb_recv,
    fwd_send,
    fwd_recv,
    h_send,
    h_recv,
    d_send,
    d_recv,
    w_send,
    w_recv,
    v_send,
    v_recv,
):
    a = lax.axis_index("aux")
    r = lax.axis_index("row")
    naux, nb, kept, bs, _ = ints.shape
    own = nb * bs
    half = aux // 2
    quota = out_ref.shape[0]
    core = lax.rem(a, 2)
    sibling = a + 1 - 2 * core
    low = a < half
    g = jnp.where(low, 0, 2)
    has_left = r > 0
    has_right = r < rows - 1
    source_row = jnp.where(low, r - 1, r + 1)
    target_row = jnp.where(low, r + 1, r - 1)
    has_source = jnp.where(low, r, rows - 1 - r) > 0
    has_target = jnp.where(low, rows - 1 - r, r) > 0
    slots = (1, 2 - g, g)
    ext = (e0, e1, e2)
    held = (h0, h1, h2)
    came = (rh0, rh1)

    load = pltpu.make_async_copy(int_hbm, ints, int_sem)
    load.start()

    barrier = pltpu.get_barrier_semaphore()

    def greet(device):
        pl.semaphore_signal(barrier, inc=1, device_id=device, device_id_type=MESH)

    @pl.when(has_left)
    def _():
        greet((a, r - 1))

    @pl.when(has_right)
    def _():
        greet((a, r + 1))

    for step in range(1, aux):
        greet((lax.rem(a + step, aux), r))

    @pl.when(has_source)
    def _():
        for place in range(half):
            greet((jnp.where(low, half + place, place), source_row))

    greeted = jnp.where(has_left, 1, 0) + jnp.where(has_right, 1, 0)
    greeted += jnp.where(has_source, half, 0) + aux - 1
    pl.semaphore_wait(barrier, greeted)

    def remote(src, dst, send, recv, device):
        return pltpu.make_async_remote_copy(
            src_ref=src,
            dst_ref=dst,
            send_sem=send,
            recv_sem=recv,
            device_id=device,
            device_id_type=MESH,
        )

    def orb_right(i):
        return remote(
            orb_ref.at[slots[i] + 2, core],
            ext[i].at[core],
            orb_send.at[i, 0],
            orb_recv.at[i, 0],
            (a, r + 1),
        )

    def orb_left(i):
        return remote(
            orb_ref.at[slots[i], core],
            ext[i].at[2 * nb + core],
            orb_send.at[i, 1],
            orb_recv.at[i, 1],
            (a, r - 1),
        )

    def forward(i, side):
        block = ext[i].at[2 * nb * side + core]
        return remote(block, block, fwd_send.at[i, side], fwd_recv.at[i, side], (sibling, r))

    def forwarded(i, side):
        block = ext[i].at[2 * nb * side + 1 - core]
        return remote(block, block, fwd_send.at[i, side], fwd_recv.at[i, side], (sibling, r))

    def send_orbitals(i):
        @pl.when(has_right)
        def _():
            orb_right(i).start()

        @pl.when(has_left)
        def _():
            orb_left(i).start()

    def share_orbitals(i):
        ext[i][nb : 2 * nb] = orb_ref[slots[i] + 1]

        @pl.when(has_left)
        def _():
            orb_right(i).wait_recv()
            forward(i, 0).start()

        @pl.when(has_right)
        def _():
            orb_left(i).wait_recv()
            forward(i, 1).start()

    def await_orbitals(i):
        @pl.when(has_left)
        def _():
            forwarded(i, 0).wait_recv()

        @pl.when(has_right)
        def _():
            forwarded(i, 1).wait_recv()

    def transform(i, b):
        factor = mask_ref[b, slots[i]]
        columns = [cols_ref[b, k] for k in range(kept)]

        @pl.loop(0, naux)
        def _(p):
            total = jnp.zeros((bs, held[i].shape[-1]), jnp.float32)
            for k in range(kept):
                total += jnp.dot(
                    ints[p, b, k], ext[i][columns[k]], preferred_element_type=jnp.float32
                )
            held[i][b, p] = (total * factor).astype(jnp.bfloat16)

    def half_copy(i, b):
        return remote(
            held[i].at[b], came[i].at[b], h_send.at[i, b], h_recv.at[i, b], (a, target_row)
        )

    def send_half(i, b):
        @pl.when(has_target)
        def _():
            half_copy(i, b).start()

    def product(pairs):
        def add(p, total):
            for left, lb, right, rb in pairs:
                total += lax.dot_general(
                    left[lb, p], right[rb, p], NT, preferred_element_type=jnp.float32
                )
            return total

        return lax.fori_loop(0, naux, add, jnp.zeros((bs, bs), jnp.float32)) * scale

    def part_of(owner, base, start, stop):
        return overlap(base + start, base + stop, owner * quota, (owner + 1) * quota)

    def diagonal_copy(owner, contributor, span):
        lo, hi = span
        return remote(
            d_buf.at[pl.ds(lo - own, hi - lo)],
            s_rec.at[contributor, pl.ds(lo - owner * quota, hi - lo)],
            d_send.at[owner],
            d_recv.at[contributor],
            (owner, r),
        )

    def beside_copy(owner, contributor, span, base, b):
        lo, hi = span
        return remote(
            w_buf.at[b, pl.ds(lo - base - b * bs, hi - lo)],
            s_rec.at[contributor, pl.ds(lo - owner * quota, hi - lo)],
            w_send.at[owner, b],
            w_recv.at[contributor, b],
            (owner, r),
        )

    def turned_copy(owner, place, span, base, b):
        lo, hi = span
        return remote(
            v_buf.at[b, pl.ds(lo - base, hi - lo)],
            v_rec.at[place, b, pl.ds(lo - owner * quota, hi - lo)],
            v_send.at[owner, b],
            v_recv.at[place, b],
            (owner, source_row),
        )

    def each_diagonal(act):
        for owner in range(aux):
            span = part_of(owner, own, 0, own)
            if span is not None:

                @pl.when(a != owner)
                def _():
                    act(diagonal_copy(owner, a, span))

    def each_beside(b, act):
        for in_low, base in ((True, 0), (False, 2 * own)):

            @pl.when(jnp.logical_and(has_source, low if in_low else jnp.logical_not(low)))
            def _():
                for owner in range(aux):
                    span = part_of(owner, base, b * bs, (b + 1) * bs)
                    if span is not None:

                        @pl.when(a != owner)
                        def _():
                            act(beside_copy(owner, a, span, base, b))

    def each_turned(b, act):
        for in_low, base in ((True, 2 * own), (False, 0)):

            @pl.when(jnp.logical_and(has_source, low if in_low else jnp.logical_not(low)))
            def _():
                for owner in range(aux):
                    span = part_of(owner, base, 0, own)
                    if span is not None:
                        act(turned_copy(owner, lax.rem(a, half), span, base, b))

    def start(copy):
        copy.start()

    def wait_send(copy):
        copy.wait_send()

    send_orbitals(0)
    send_orbitals(1)
    share_orbitals(0)
    load.wait()
    await_orbitals(0)
    transform(0, 0)
    send_half(0, 0)
    share_orbitals(1)
    transform(0, 1)
    await_orbitals(1)
    transform(1, 0)
    send_half(1, 0)
    send_orbitals(2)
    transform(1, 1)
    for i in range(2):
        send_half(i, 1)
    share_orbitals(2)
    await_orbitals(2)
    for b in range(nb):
        transform(2, b)

    for b in range(nb):
        for other in range(nb):
            d_buf[b * bs : (b + 1) * bs, other * bs : (other + 1) * bs] = product(
                [(h, b, h, other) for h in held]
            )
    each_diagonal(start)

    for b in range(nb):

        @pl.when(has_source)
        def _():
            half_copy(0, b).wait_recv()
            half_copy(1, b).wait_recv()
            for other in range(nb):
                v_buf[b, other * bs : (other + 1) * bs] = product(
                    [(h2, other, rh0, b), (h0, other, rh1, b)]
                ).astype(jnp.bfloat16)

        each_turned(b, start)

        @pl.when(has_source)
        def _():
            for other in range(nb):
                w_buf[b, :, other * bs : (other + 1) * bs] = product(
                    [(rh0, b, h2, other), (rh1, b, h0, other)]
                )

        each_beside(b, start)

    for owner in range(aux):

        @pl.when(a == owner)
        def _():
            first = owner * quota
            span = part_of(owner, own, 0, own)
            if span is not None:
                lo, hi = span
                total = d_buf[lo - own : hi - own]
                for peer in range(aux):
                    if peer != owner:
                        diagonal_copy(owner, peer, span).wait_recv()
                        total += s_rec[peer, lo - first : hi - first]
                out_ref[lo - first : hi - first] = total
            base = 0 if owner < half else 2 * own
            group = range(half) if owner < half else range(half, aux)
            whole = part_of(owner, base, 0, own)
            if whole is not None:

                @pl.when(jnp.logical_not(has_source))
                def _():
                    lo, hi = whole
                    out_ref[lo - first : hi - first] = jnp.zeros(
                        (hi - lo, out_ref.shape[1]), jnp.float32
                    )

                @pl.when(has_source)
                def _():
                    for b in range(nb):
                        span = part_of(owner, base, b * bs, (b + 1) * bs)
                        if span is not None:
                            lo, hi = span
                            shift = base + b * bs
                            total = w_buf[b, lo - shift : hi - shift]
                            for peer in group:
                                if peer != owner:
                                    beside_copy(owner, peer, span, base, b).wait_recv()
                                    total += s_rec[peer, lo - first : hi - first]
                            out_ref[lo - first : hi - first] = total
                    lo, hi = whole
                    for b in range(nb):
                        for place in range(half):
                            turned_copy(owner, place, whole, base, b).wait_recv()
                            out_ref[lo - first : hi - first, b * bs : (b + 1) * bs] += v_rec[
                                place, b, lo - first : hi - first
                            ].astype(jnp.float32)

    for i in range(3):

        @pl.when(has_right)
        def _():
            orb_right(i).wait_send()
            forward(i, 1).wait_send()

        @pl.when(has_left)
        def _():
            orb_left(i).wait_send()
            forward(i, 0).wait_send()

    @pl.when(has_target)
    def _():
        for i in range(2):
            for b in range(nb):
                half_copy(i, b).wait_send()

    each_diagonal(wait_send)
    for b in range(nb):
        each_turned(b, wait_send)
        each_beside(b, wait_send)


def on_device(integrals, block_columns, orbitals, occ_mask):
    naux, nb, kept, bs, _ = integrals.shape
    own, occ_count = orbitals.shape
    aux = lax.axis_size("aux")
    rows = lax.axis_size("row")
    r = lax.axis_index("row")
    width = occ_count // rows
    scale = 1.0 / (naux * aux * width) ** 0.5
    quota = 3 * own // aux
    near = [
        lax.dynamic_slice_in_dim(orbitals, jnp.clip(r + step, 0, rows - 1) * width, width, 1)
        for step in range(-2, 3)
    ]
    orb = jnp.stack(near, 0).reshape(5, nb, bs, width)
    cols = block_columns - (r - 1) * nb
    slices = r - 1 + jnp.arange(3)
    inside = (slices >= 0) & (slices < rows)
    mask_rows = lax.dynamic_slice_in_dim(occ_mask, r * nb, nb, 0).astype(jnp.float32)
    mask = mask_rows[:, jnp.clip(slices, 0, rows - 1)] * inside.astype(jnp.float32)[None]
    ext = pltpu.VMEM((3 * nb, bs, width), jnp.bfloat16)
    held = pltpu.VMEM((nb, naux, bs, width), jnp.bfloat16)
    dma = pltpu.SemaphoreType.DMA
    flops = 2 * naux * bs * bs * width * nb * (3 * kept + 7 * nb)
    turned = pl.pallas_call(
        functools.partial(kernel, aux, rows, scale),
        out_shape=jax.ShapeDtypeStruct((quota, own), jnp.float32),
        in_specs=[
            pl.BlockSpec(memory_space=pltpu.SMEM),
            pl.BlockSpec(memory_space=pltpu.SMEM),
            pl.BlockSpec(memory_space=pltpu.VMEM),
            pl.BlockSpec(memory_space=pl.ANY),
        ],
        out_specs=pl.BlockSpec(memory_space=pltpu.VMEM),
        scratch_shapes=[pltpu.VMEM(integrals.shape, jnp.bfloat16)]
        + [ext] * 3
        + [held] * 5
        + [
            pltpu.VMEM((own, own), jnp.float32),
            pltpu.VMEM((nb, bs, own), jnp.float32),
            pltpu.VMEM((nb, own, bs), jnp.bfloat16),
            pltpu.VMEM((aux, quota, own), jnp.float32),
            pltpu.VMEM((aux // 2, nb, quota, bs), jnp.bfloat16),
            dma,
            dma((3, 2)),
            dma((3, 2)),
            dma((3, 2)),
            dma((3, 2)),
            dma((2, nb)),
            dma((2, nb)),
            dma((aux,)),
            dma((aux,)),
            dma((aux, nb)),
            dma((aux, nb)),
            dma((aux, nb)),
            dma((aux // 2, nb)),
        ],
        compiler_params=pltpu.CompilerParams(
            collective_id=0, has_side_effects=True, vmem_limit_bytes=48 * 1024 * 1024
        ),
        cost_estimate=pl.CostEstimate(
            flops=flops, bytes_accessed=2 * integrals.size, transcendentals=0
        ),
    )(cols, mask, orb, integrals)
    return turned.T


def solution(mesh):
    in_specs = (P("aux", "row", None, None, None), P("row", None), P("row", None), P())
    out_specs = P("row", "aux")
    return jax.shard_map(
        on_device, mesh=mesh, in_specs=in_specs, out_specs=out_specs, check_vma=False
    )
```

time: 389 us -> 102 us (0.26)
  the two profiles are of different devices: /device:TPU:13 before, /device:TPU:11 now
where the time goes in v1:
time: 102 us
  Pallas kernels  97.8 us (96%)
  local copies, waits for them, and re-layouts  3.8 us (4%)
    pallas_call x1, Pallas kernels, on_device(): pl.pallas_call(functools.partial(kernel, aux, rows, scale), out_shape=jax...  97.8 us

profile of v1, /device:TPU:11, one launch (start us, length us, event | category | flops | bytes accessed | tf_op | source)
XLA Modules:
  0.0 101.7 jit_solution(2648283513654177418)
XLA Ops:
  0.0 1.4 %constant_dynamic-slice_fusion = (bf16[512,256]{1,0:T(8,128)(2,1)S(1)}, bf16[512,256]{1,0:T(8,128)(2,1)S(1)}, bf16[512,256]{1,0:T(8,128)(2,1)S(1)}, bf16[512,256]{1,0:T(8,128)(2,1)S(1)}, bf16[512,256]{1,0:T(8,128)(2,1)S(1)}) fusion(bf16[512,2048]{1,0:T(8,128)(2,1)} %param.6, s32[]{:T(128)S(6)} %select_n.34, s32[]{:T(128)S(6)} %select_n.32, s32[]{:T(128)S(6)} %select_n.31, ...), kind=kLoop, calls=%fused_computation.10 | loop fusion | bytes 2621460 | tf_op jit(solution)/shard_map/dynamic_slice | solution.py:407
  1.4 0.0 copy-start
  1.4 0.0 copy-start.1
  1.5 0.5 copy-done
  2.1 0.1 dynamic-slice_convert_fusion
  2.2 0.6 gather_fusion
  2.7 0.1 copy.5
  2.8 0.0 copy-done.1
  2.8 97.8 %shard_map.46 = f32[384,512]{1,0:T(8,128)S(1)} custom-call(s32[2,4]{1,0:T(2,128)S(1)} %broadcast_subtract_fusion.cols_ref, f32[2,3]{1,0:T(2,128)S(1)} %multiply_bitcast_fusion.mask_ref, bf16[5,2,256,256]{3,2,1,0:T(8,128)(2,1)S(1)} %constant_dynamic-update-slice_fusion.orb_ref, bf16[4,2,4,256,256]{4,3,2,1,0:T(8,128)(2,1)} %int_hbm.1), custom_call_target="tpu_custom_call" | custom-call | flops 6979321856 | bytes 4194304 | tf_op jit(solution)/shard_map/pallas_call | solution.py:420
  100.6 1.1 %copy.6 = f32[512,384]{1,0:T(8,128)} copy(f32[512,384]{0,1:T(8,128)S(1)} %bitcast.10) | data formatting | bytes 1572864 | tf_op jit(solution)/shard_map/transpose | solution.py:460
  (10 shorter events, 0.1 us)
Async XLA Ops:
  1.4 0.7 copy-start
  1.4 1.4 %copy-start.1 = (s32[2,4]{1,0:T(2,128)S(1)}, s32[2,4]{1,0:T(2,128)}, u32[]{:S(2)}) copy-start(s32[2,4]{1,0:T(2,128)} %param.5) | copy-start | bytes 100

commit v2 on v1

v2 whole, which is shorter than its diff:
```python
import functools

import jax
import jax.numpy as jnp
from jax import lax
from jax.experimental import pallas as pl
from jax.experimental.pallas import tpu as pltpu
from jax.sharding import PartitionSpec as P

MESH = pl.DeviceIdType.MESH
NT = (((1,), (1,)), ((), ()))


def overlap(lo, hi, start, stop):
    lo, hi = max(lo, start), min(hi, stop)
    return (lo, hi) if lo < hi else None


def kernel(
    aux,
    rows,
    scale,
    cols_ref,
    mask_ref,
    orb_hbm,
    int_hbm,
    out_ref,
    ints,
    orb_ref,
    e0,
    e1,
    e2,
    h0,
    h1,
    h2,
    rh0,
    rh1,
    d_buf,
    w_buf,
    v_buf,
    s_rec,
    v_rec,
    int_sem,
    near_sem,
    orb_send,
    orb_recv,
    fwd_send,
    fwd_recv,
    h_send,
    h_recv,
    d_send,
    d_recv,
    w_send,
    w_recv,
    v_send,
    v_recv,
):
    a = lax.axis_index("aux")
    r = lax.axis_index("row")
    naux, nb, kept, bs, _ = ints.shape
    own = nb * bs
    width = e0.shape[-1]
    share = own // aux
    per_block = bs // share
    piece = w_buf.shape[1]
    chunks = own // piece
    half = aux // 2
    quota = out_ref.shape[0]
    low = a < half
    has_left = r > 0
    has_right = r < rows - 1
    source_row = jnp.where(low, r - 1, r + 1)
    target_row = jnp.where(low, r + 1, r - 1)
    has_source = jnp.where(low, r, rows - 1 - r) > 0
    has_target = jnp.where(low, rows - 1 - r, r) > 0
    ext = (e0, e1, e2)
    held = (h0, h1, h2)
    came = (rh0, rh1)

    load = pltpu.make_async_copy(int_hbm, ints, int_sem)
    load.start()
    near = []
    for t in range(5):
        if len(orb_hbm.shape) == 2:
            column = jnp.clip(r - 2 + t, 0, rows - 1) * width
            source = orb_hbm.at[:, pl.ds(pl.multiple_of(column, width), width)]
        else:
            source = orb_hbm.at[t]
        near.append(pltpu.make_async_copy(source, orb_ref.at[t], near_sem.at[t]))
        near[t].start()

    barrier = pltpu.get_barrier_semaphore()

    def greet(device):
        pl.semaphore_signal(barrier, inc=1, device_id=device, device_id_type=MESH)

    @pl.when(has_left)
    def _():
        greet((a, r - 1))

    @pl.when(has_right)
    def _():
        greet((a, r + 1))

    for step in range(1, aux):
        greet((lax.rem(a + step, aux), r))

    @pl.when(has_source)
    def _():
        for place in range(half):
            greet((jnp.where(low, half + place, place), source_row))

    greeted = jnp.where(has_left, 1, 0) + jnp.where(has_right, 1, 0)
    greeted += jnp.where(has_source, half, 0) + aux - 1
    pl.semaphore_wait(barrier, greeted)

    def remote(src, dst, send, recv, device):
        return pltpu.make_async_remote_copy(
            src_ref=src,
            dst_ref=dst,
            send_sem=send,
            recv_sem=recv,
            device_id=device,
            device_id_type=MESH,
        )

    def quarter(i, side, contributor):
        first = pl.multiple_of(lax.rem(contributor, per_block) * share, share)
        return ext[i].at[2 * nb * side + contributor // per_block, pl.ds(first, share)]

    mine = pl.ds(pl.multiple_of(a * share, share), share)

    def orb_right(i):
        return remote(
            orb_ref.at[i + 2, mine],
            quarter(i, 0, a),
            orb_send.at[i, 0],
            orb_recv.at[i, 0],
            (a, r + 1),
        )

    def orb_left(i):
        return remote(
            orb_ref.at[i, mine],
            quarter(i, 1, a),
            orb_send.at[i, 1],
            orb_recv.at[i, 1],
            (a, r - 1),
        )

    def forward(i, side, step, contributor):
        block = quarter(i, side, contributor)
        return remote(
            block,
            block,
            fwd_send.at[i, side, step - 1],
            fwd_recv.at[i, side, step - 1],
            (lax.rem(a + step, aux), r),
        )

    def send_orbitals(i):
        @pl.when(has_right)
        def _():
            orb_right(i).start()

        @pl.when(has_left)
        def _():
            orb_left(i).start()

    def share_orbitals(i):
        @pl.when(has_left)
        def _():
            orb_right(i).wait_recv()
            for step in range(1, aux):
                forward(i, 0, step, a).start()

        @pl.when(has_right)
        def _():
            orb_left(i).wait_recv()
            for step in range(1, aux):
                forward(i, 1, step, a).start()

        for b in range(nb):
            ext[i][nb + b] = orb_ref[i + 1, b * bs : (b + 1) * bs]

    def await_orbitals(i):
        for side, there in ((0, has_left), (1, has_right)):

            @pl.when(there)
            def _():
                for step in range(1, aux):
                    forward(i, side, step, lax.rem(a + aux - step, aux)).wait_recv()

    def by_half(i, act):
        if i == 0:
            act(1)
        else:

            @pl.when(low)
            def _():
                act(4 - 2 * i)

            @pl.when(jnp.logical_not(low))
            def _():
                act(2 * i - 2)

    def transform(i, b):
        by_half(i, lambda slot: transform_slot(i, slot, b))

    def transform_slot(i, slot, b):
        at = r - 1 + slot
        inside = jnp.logical_and(at >= 0, at < rows)
        held_here = mask_ref[r * nb + b, jnp.clip(at, 0, rows - 1)]
        factor = jnp.where(inside, held_here, 0).astype(jnp.float32)
        columns = [jnp.clip(cols_ref[b, k] - (r - 1) * nb, 0, 3 * nb - 1) for k in range(kept)]

        @pl.loop(0, naux)
        def _(p):
            total = jnp.zeros((bs, held[i].shape[-1]), jnp.float32)
            for k in range(kept):
                total += jnp.dot(
                    ints[p, b, k], ext[slot][columns[k]], preferred_element_type=jnp.float32
                )
            held[i][b, p] = (total * factor).astype(jnp.bfloat16)

    def piece_of(c):
        start = c * piece % bs
        return c * piece // bs, slice(start, start + piece)

    def half_copy(i, c):
        b, inner = piece_of(c)
        inner = pl.ds(inner.start, piece)
        return remote(
            held[i].at[b, :, inner],
            came[i].at[b, :, inner],
            h_send.at[i, c],
            h_recv.at[i, c],
            (a, target_row),
        )

    def send_half(i, b):
        @pl.when(has_target)
        def _():
            for c in range(b * bs // piece, (b + 1) * bs // piece):
                half_copy(i, c).start()

    def product(pairs, shape):
        def add(p, total):
            for left, lb, li, right, rb, ri in pairs:
                total += lax.dot_general(
                    left[lb, p, li], right[rb, p, ri], NT, preferred_element_type=jnp.float32
                )
            return total

        return lax.fori_loop(0, naux, add, jnp.zeros(shape, jnp.float32)) * scale

    def part_of(owner, base, start, stop):
        return overlap(base + start, base + stop, owner * quota, (owner + 1) * quota)

    def diagonal_copy(owner, contributor, span):
        lo, hi = span
        return remote(
            d_buf.at[pl.ds(lo - own, hi - lo)],
            s_rec.at[contributor, pl.ds(lo - owner * quota, hi - lo)],
            d_send.at[owner],
            d_recv.at[contributor],
            (owner, r),
        )

    def beside_copy(owner, contributor, span, base, b):
        lo, hi = span
        return remote(
            w_buf.at[b, pl.ds(lo - base - b * piece, hi - lo)],
            s_rec.at[contributor, pl.ds(lo - owner * quota, hi - lo)],
            w_send.at[owner, b],
            w_recv.at[contributor, b],
            (owner, r),
        )

    def turned_copy(owner, place, span, base, b):
        lo, hi = span
        return remote(
            v_buf.at[b, pl.ds(lo - base, hi - lo)],
            v_rec.at[place, b, pl.ds(lo - owner * quota, hi - lo)],
            v_send.at[owner, b],
            v_recv.at[place, b],
            (owner, source_row),
        )

    def each_diagonal(act):
        for owner in range(aux):
            span = part_of(owner, own, 0, own)
            if span is not None:

                @pl.when(a != owner)
                def _():
                    act(diagonal_copy(owner, a, span))

    def each_beside(b, act):
        for in_low, base in ((True, 0), (False, 2 * own)):

            @pl.when(jnp.logical_and(has_source, low if in_low else jnp.logical_not(low)))
            def _():
                for owner in range(aux):
                    span = part_of(owner, base, b * piece, (b + 1) * piece)
                    if span is not None:

                        @pl.when(a != owner)
                        def _():
                            act(beside_copy(owner, a, span, base, b))

    def each_turned(b, act):
        for in_low, base in ((True, 2 * own), (False, 0)):

            @pl.when(jnp.logical_and(has_source, low if in_low else jnp.logical_not(low)))
            def _():
                for owner in range(aux):
                    span = part_of(owner, base, 0, own)
                    if span is not None:
                        act(turned_copy(owner, lax.rem(a, half), span, base, b))

    def start(copy):
        copy.start()

    def wait_send(copy):
        copy.wait_send()

    for copy in near:
        copy.wait()
    for slot in (1, 0, 2):
        send_orbitals(slot)
    for slot in (1, 0, 2):
        share_orbitals(slot)
    load.wait()
    by_half(0, await_orbitals)
    transform(0, 0)
    send_half(0, 0)
    by_half(1, await_orbitals)
    transform(1, 0)
    send_half(1, 0)
    for b in range(1, nb):
        for i in range(2):
            transform(i, b)
            send_half(i, b)
    by_half(2, await_orbitals)
    for b in range(nb):
        transform(2, b)

    full = slice(0, bs)
    for b in range(nb):
        for other in range(nb):
            d_buf[b * bs : (b + 1) * bs, other * bs : (other + 1) * bs] = product(
                [(h, b, full, h, other, full) for h in held], (bs, bs)
            )
    each_diagonal(start)

    for c in range(chunks):
        b, inner = piece_of(c)

        @pl.when(has_source)
        def _():
            half_copy(0, c).wait_recv()
            half_copy(1, c).wait_recv()
            for other in range(nb):
                v_buf[c, other * bs : (other + 1) * bs] = product(
                    [(h2, other, full, rh0, b, inner), (h0, other, full, rh1, b, inner)],
                    (bs, piece),
                ).astype(jnp.bfloat16)

        each_turned(c, start)

        @pl.when(has_source)
        def _():
            for other in range(nb):
                w_buf[c, :, other * bs : (other + 1) * bs] = product(
                    [(rh0, b, inner, h2, other, full), (rh1, b, inner, h0, other, full)],
                    (piece, bs),
                )

        each_beside(c, start)

    for owner in range(aux):

        @pl.when(a == owner)
        def _():
            first = owner * quota
            span = part_of(owner, own, 0, own)
            if span is not None:
                lo, hi = span
                total = d_buf[lo - own : hi - own]
                for peer in range(aux):
                    if peer != owner:
                        diagonal_copy(owner, peer, span).wait_recv()
                        total += s_rec[peer, lo - first : hi - first]
                out_ref[lo - first : hi - first] = total
            base = 0 if owner < half else 2 * own
            group = range(half) if owner < half else range(half, aux)
            whole = part_of(owner, base, 0, own)
            if whole is not None:

                @pl.when(jnp.logical_not(has_source))
                def _():
                    lo, hi = whole
                    out_ref[lo - first : hi - first] = jnp.zeros(
                        (hi - lo, out_ref.shape[1]), jnp.float32
                    )

                @pl.when(has_source)
                def _():
                    for b in range(chunks):
                        span = part_of(owner, base, b * piece, (b + 1) * piece)
                        if span is not None:
                            lo, hi = span
                            shift = base + b * piece
                            total = w_buf[b, lo - shift : hi - shift]
                            for peer in group:
                                if peer != owner:
                                    beside_copy(owner, peer, span, base, b).wait_recv()
                                    total += s_rec[peer, lo - first : hi - first]
                            out_ref[lo - first : hi - first] = total
                    lo, hi = whole
                    for b in range(chunks):
                        for place in range(half):
                            turned_copy(owner, place, whole, base, b).wait_recv()
                            out_ref[lo - first : hi - first, b * piece : (b + 1) * piece] += v_rec[
                                place, b, lo - first : hi - first
                            ].astype(jnp.float32)

    for i in range(3):
        for side, there, copy in ((0, has_left, orb_left), (1, has_right, orb_right)):

            @pl.when(there)
            def _():
                copy(i).wait_send()
                for step in range(1, aux):
                    forward(i, side, step, a).wait_send()

    @pl.when(has_target)
    def _():
        for i in range(2):
            for c in range(chunks):
                half_copy(i, c).wait_send()

    each_diagonal(wait_send)
    for c in range(chunks):
        each_turned(c, wait_send)
        each_beside(c, wait_send)


def on_device(integrals, block_columns, orbitals, occ_mask):
    naux, nb, kept, bs, _ = integrals.shape
    own, occ_count = orbitals.shape
    aux = lax.axis_size("aux")
    rows = lax.axis_size("row")
    r = lax.axis_index("row")
    width = occ_count // rows
    scale = 1.0 / (naux * aux * width) ** 0.5
    quota = 3 * own // aux
    piece = bs // 2
    chunks = own // piece
    if width % 128:
        near = [
            lax.dynamic_slice_in_dim(orbitals, jnp.clip(r + step, 0, rows - 1) * width, width, 1)
            for step in range(-2, 3)
        ]
        orbitals = jnp.stack(near, 0)
    ext = pltpu.VMEM((3 * nb, bs, width), jnp.bfloat16)
    held = pltpu.VMEM((nb, naux, bs, width), jnp.bfloat16)
    dma = pltpu.SemaphoreType.DMA
    flops = 2 * naux * bs * bs * width * nb * (3 * kept + 7 * nb)
    turned = pl.pallas_call(
        functools.partial(kernel, aux, rows, scale),
        out_shape=jax.ShapeDtypeStruct((quota, own), jnp.float32),
        in_specs=[
            pl.BlockSpec(memory_space=pltpu.SMEM),
            pl.BlockSpec(memory_space=pltpu.SMEM),
            pl.BlockSpec(memory_space=pl.ANY),
            pl.BlockSpec(memory_space=pl.ANY),
        ],
        out_specs=pl.BlockSpec(memory_space=pltpu.VMEM),
        scratch_shapes=[
            pltpu.VMEM(integrals.shape, jnp.bfloat16),
            pltpu.VMEM((5, own, width), jnp.bfloat16),
        ]
        + [ext] * 3
        + [held] * 5
        + [
            pltpu.VMEM((own, own), jnp.float32),
            pltpu.VMEM((chunks, piece, own), jnp.float32),
            pltpu.VMEM((chunks, own, piece), jnp.bfloat16),
            pltpu.VMEM((aux, quota, own), jnp.float32),
            pltpu.VMEM((aux // 2, chunks, quota, piece), jnp.bfloat16),
            dma,
            dma((5,)),
            dma((3, 2)),
            dma((3, 2)),
            dma((3, 2, aux - 1)),
            dma((3, 2, aux - 1)),
            dma((2, chunks)),
            dma((2, chunks)),
            dma((aux,)),
            dma((aux,)),
            dma((aux, chunks)),
            dma((aux, chunks)),
            dma((aux, chunks)),
            dma((aux // 2, chunks)),
        ],
        compiler_params=pltpu.CompilerParams(
            collective_id=0, has_side_effects=True, vmem_limit_bytes=48 * 1024 * 1024
        ),
        cost_estimate=pl.CostEstimate(
            flops=flops, bytes_accessed=2 * integrals.size, transcendentals=0
        ),
    )(block_columns, occ_mask, orbitals, integrals)
    return turned.T


def solution(mesh):
    in_specs = (P("aux", "row", None, None, None), P("row", None), P("row", None), P())
    out_specs = P("row", "aux")
    return jax.shard_map(
        on_device, mesh=mesh, in_specs=in_specs, out_specs=out_specs, check_vma=False
    )
```

time: 102 us -> 90.1 us (0.88)
  Pallas kernels: 97.8 us -> 85.7 us
    pallas_call x1, Pallas kernels: 97.8 us -> 85.7 us  [on_device(): pl.pallas_call(functools.partial(kernel, aux, rows, scale), out_shape=jax...]
    unnamed x8 -> x5, local copies, waits for them, and re-layouts: 0.61 us -> 3.03 us
    dynamic_slice x1 -> x0, local copies, waits for them, and re-layouts: 1.37 us -> none  [on_device(): lax.dynamic_slice_in_dim(orbitals, jnp.clip(r + step, 0, rows - 1) * widt...]
where the time goes in v2:
time: 90.1 us; the launch traced here: 89.9 us
  Pallas kernels  85.7 us (95%)
  local copies, waits for them, and re-layouts  4.18 us (5%)
    pallas_call x1, Pallas kernels, on_device(): pl.pallas_call(functools.partial(kernel, aux, rows, scale), out_shape=jax...  85.7 us
    unnamed x5, local copies, waits for them, and re-layouts  3.03 us

profile of v2, /device:TPU:11, one launch (start us, length us, event | category | flops | bytes accessed | tf_op | source)
XLA Modules:
  0.0 89.9 jit_solution(441945166797304130)
XLA Ops:
  0.0 0.8 copy.5.mask_ref
  0.8 0.0 copy-start
  0.8 1.6 %copy-done = bf16[512,2048]{1,0:T(8,128)(2,1)S(1)} copy-done((bf16[512,2048]{1,0:T(8,128)(2,1)S(1)}, bf16[512,2048]{1,0:T(8,128)(2,1)}, u32[]{:S(2)}) %copy-start) | copy-done | bytes 2097176
  2.3 0.0 copy-start.1
  2.4 0.7 copy-done.1
  3.0 85.7 %shard_map.46 = f32[384,512]{1,0:T(8,128)S(1)} custom-call(s32[2,4]{1,0:T(2,128)S(1)} %copy-done.1, s32[16,8]{1,0:T(8,128)S(1)} %copy.5.mask_ref, bf16[512,2048]{1,0:T(8,128)(2,1)S(1)} %copy-done, bf16[4,2,4,256,256]{4,3,2,1,0:T(8,128)(2,1)} %int_hbm.1), custom_call_target="tpu_custom_call" | custom-call | flops 6979321856 | bytes 4194304 | tf_op jit(solution)/shard_map/pallas_call | solution.py:471
  88.8 1.1 %copy.6 = f32[512,384]{1,0:T(8,128)} copy(f32[512,384]{0,1:T(8,128)S(1)} %bitcast.1) | data formatting | bytes 1572864 | tf_op jit(solution)/shard_map/transpose | solution.py:515
Async XLA Ops:
  0.8 1.6 %copy-start = (bf16[512,2048]{1,0:T(8,128)(2,1)S(1)}, bf16[512,2048]{1,0:T(8,128)(2,1)}, u32[]{:S(2)}) copy-start(bf16[512,2048]{1,0:T(8,128)(2,1)} %orb_hbm.1) | copy-start | bytes 6291460
  2.3 0.7 copy-start.1

commit v3 on v2

--- a/solution.py
+++ b/solution.py
@@ -20,11 +20,13 @@
     aux,
     rows,
     scale,
-    cols_ref,
-    mask_ref,
+    cols_hbm,
+    mask_hbm,
     orb_hbm,
     int_hbm,
     out_ref,
+    cols_ref,
+    mask_ref,
     ints,
     orb_ref,
     e0,
@@ -41,6 +43,7 @@
     s_rec,
     v_rec,
     int_sem,
+    small_sem,
     near_sem,
     orb_send,
     orb_recv,
@@ -79,6 +82,12 @@
 
     load = pltpu.make_async_copy(int_hbm, ints, int_sem)
     load.start()
+    small = [
+        pltpu.make_async_copy(cols_hbm, cols_ref, small_sem.at[0]),
+        pltpu.make_async_copy(mask_hbm, mask_ref, small_sem.at[1]),
+    ]
+    for copy in small:
+        copy.start()
     near = []
     for t in range(5):
         if len(orb_hbm.shape) == 2:
@@ -327,21 +336,27 @@
 
     for copy in near:
         copy.wait()
-    for slot in (1, 0, 2):
+    send_orbitals(1)
+    share_orbitals(1)
+    for slot in (0, 2):
         send_orbitals(slot)
-    for slot in (1, 0, 2):
-        share_orbitals(slot)
     load.wait()
-    by_half(0, await_orbitals)
+    for copy in small:
+        copy.wait()
+    await_orbitals(1)
     transform(0, 0)
     send_half(0, 0)
+    for slot in (0, 2):
+        share_orbitals(slot)
+    for b in range(1, nb):
+        transform(0, b)
     by_half(1, await_orbitals)
     transform(1, 0)
     send_half(1, 0)
     for b in range(1, nb):
-        for i in range(2):
-            transform(i, b)
-            send_half(i, b)
+        send_half(0, b)
+        transform(1, b)
+        send_half(1, b)
     by_half(2, await_orbitals)
     for b in range(nb):
         transform(2, b)
@@ -354,6 +369,60 @@
             )
     each_diagonal(start)
 
+    def finish_diagonal():
+        for owner in range(aux):
+            span = part_of(owner, own, 0, own)
+            if span is not None:
+
+                @pl.when(a == owner)
+                def _():
+                    lo, hi = span
+                    first = owner * quota
+                    total = d_buf[lo - own : hi - own]
+                    for peer in range(aux):
+                        if peer != owner:
+                            diagonal_copy(owner, peer, span).wait_recv()
+                            total += s_rec[peer, lo - first : hi - first]
+                    out_ref[lo - first : hi - first] = total
+
+    def side_of(owner):
+        return (0, range(half)) if owner < half else (2 * own, range(half, aux))
+
+    def finish_beside(c):
+        for owner in range(aux):
+            base, group = side_of(owner)
+            span = part_of(owner, base, c * piece, (c + 1) * piece)
+            if span is not None:
+
+                @pl.when(jnp.logical_and(a == owner, has_source))
+                def _():
+                    lo, hi = span
+                    first = owner * quota
+                    shift = base + c * piece
+                    total = w_buf[c, lo - shift : hi - shift]
+                    for peer in group:
+                        if peer != owner:
+                            beside_copy(owner, peer, span, base, c).wait_recv()
+                            total += s_rec[peer, lo - first : hi - first]
+                    out_ref[lo - first : hi - first] += total
+
+    def finish_turned(c):
+        for owner in range(aux):
+            base, _ = side_of(owner)
+            span = part_of(owner, base, 0, own)
+            if span is not None:
+
+                @pl.when(jnp.logical_and(a == owner, has_source))
+                def _():
+                    lo, hi = span
+                    first = owner * quota
+                    for place in range(half):
+                        turned_copy(owner, place, span, base, c).wait_recv()
+                        out_ref[lo - first : hi - first, c * piece : (c + 1) * piece] += v_rec[
+                            place, c, lo - first : hi - first
+                        ].astype(jnp.float32)
+
+    out_ref[...] = jnp.zeros_like(out_ref)
     for c in range(chunks):
         b, inner = piece_of(c)
 
@@ -378,53 +447,14 @@
                 )
 
         each_beside(c, start)
-
-    for owner in range(aux):
-
-        @pl.when(a == owner)
-        def _():
-            first = owner * quota
-            span = part_of(owner, own, 0, own)
-            if span is not None:
-                lo, hi = span
-                total = d_buf[lo - own : hi - own]
-                for peer in range(aux):
-                    if peer != owner:
-                        diagonal_copy(owner, peer, span).wait_recv()
-                        total += s_rec[peer, lo - first : hi - first]
-                out_ref[lo - first : hi - first] = total
-            base = 0 if owner < half else 2 * own
-            group = range(half) if owner < half else range(half, aux)
-            whole = part_of(owner, base, 0, own)
-            if whole is not None:
-
-                @pl.when(jnp.logical_not(has_source))
-                def _():
-                    lo, hi = whole
-                    out_ref[lo - first : hi - first] = jnp.zeros(
-                        (hi - lo, out_ref.shape[1]), jnp.float32
-                    )
-
-                @pl.when(has_source)
-                def _():
-                    for b in range(chunks):
-                        span = part_of(owner, base, b * piece, (b + 1) * piece)
-                        if span is not None:
-                            lo, hi = span
-                            shift = base + b * piece
-                            total = w_buf[b, lo - shift : hi - shift]
-                            for peer in group:
-                                if peer != owner:
-                                    beside_copy(owner, peer, span, base, b).wait_recv()
-                                    total += s_rec[peer, lo - first : hi - first]
-                            out_ref[lo - first : hi - first] = total
-                    lo, hi = whole
-                    for b in range(chunks):
-                        for place in range(half):
-                            turned_copy(owner, place, whole, base, b).wait_recv()
-                            out_ref[lo - first : hi - first, b * piece : (b + 1) * piece] += v_rec[
-                                place, b, lo - first : hi - first
-                            ].astype(jnp.float32)
+        if c == 1:
+            finish_diagonal()
+        if c >= 1:
+            finish_beside(c - 1)
+            finish_turned(c - 1)
+
+    finish_beside(chunks - 1)
+    finish_turned(chunks - 1)
 
     for i in range(3):
         for side, there, copy in ((0, has_left, orb_left), (1, has_right, orb_right)):
@@ -472,13 +502,15 @@
         functools.partial(kernel, aux, rows, scale),
         out_shape=jax.ShapeDtypeStruct((quota, own), jnp.float32),
         in_specs=[
-            pl.BlockSpec(memory_space=pltpu.SMEM),
-            pl.BlockSpec(memory_space=pltpu.SMEM),
+            pl.BlockSpec(memory_space=pl.ANY),
+            pl.BlockSpec(memory_space=pl.ANY),
             pl.BlockSpec(memory_space=pl.ANY),
             pl.BlockSpec(memory_space=pl.ANY),
         ],
         out_specs=pl.BlockSpec(memory_space=pltpu.VMEM),
         scratch_shapes=[
+            pltpu.SMEM(block_columns.shape, jnp.int32),
+            pltpu.SMEM(occ_mask.shape, jnp.int32),
             pltpu.VMEM(integrals.shape, jnp.bfloat16),
             pltpu.VMEM((5, own, width), jnp.bfloat16),
         ]
@@ -491,6 +523,7 @@
             pltpu.VMEM((aux, quota, own), jnp.float32),
             pltpu.VMEM((aux // 2, chunks, quota, piece), jnp.bfloat16),
             dma,
+            dma((2,)),
             dma((5,)),
             dma((3, 2)),
             dma((3, 2)),

time: 90.1 us -> 86.4 us (0.959)
  the two profiles are of different devices: /device:TPU:11 before, /device:TPU:13 now
where the time goes in v3:
time: 86.4 us; the launch traced here: 86.2 us
  Pallas kernels  82.1 us (95%)
  local copies, waits for them, and re-layouts  4.18 us (5%)
    pallas_call x1, Pallas kernels, on_device(): pl.pallas_call(functools.partial(kernel, aux, rows, scale), out_shape=jax...  82.1 us
    unnamed x5, local copies, waits for them, and re-layouts  3.03 us

profile of v3, /device:TPU:13, one launch (start us, length us, event | category | flops | bytes accessed | tf_op | source)
XLA Modules:
  0.0 86.2 jit_solution(15317583125074151890)
XLA Ops:
  0.0 0.8 copy.5.mask_hbm
  0.8 0.0 copy-start
  0.8 1.6 %copy-done = bf16[512,2048]{1,0:T(8,128)(2,1)S(1)} copy-done((bf16[512,2048]{1,0:T(8,128)(2,1)S(1)}, bf16[512,2048]{1,0:T(8,128)(2,1)}, u32[]{:S(2)}) %copy-start) | copy-done | bytes 2097176
  2.3 0.0 copy-start.1
  2.4 0.7 copy-done.1
  3.0 82.1 %shard_map.46 = f32[384,512]{1,0:T(8,128)S(1)} custom-call(s32[2,4]{1,0:T(2,128)S(1)} %copy-done.1, s32[16,8]{1,0:T(8,128)S(1)} %copy.5.mask_hbm, bf16[512,2048]{1,0:T(8,128)(2,1)S(1)} %copy-done, bf16[4,2,4,256,256]{4,3,2,1,0:T(8,128)(2,1)} %int_hbm.1), custom_call_target="tpu_custom_call" | custom-call | flops 6979321856 | bytes 4194304 | tf_op jit(solution)/shard_map/pallas_call | solution.py:501
  85.1 1.1 %copy.6 = f32[512,384]{1,0:T(8,128)} copy(f32[512,384]{0,1:T(8,128)S(1)} %bitcast.1) | data formatting | bytes 1572864 | tf_op jit(solution)/shard_map/transpose | solution.py:548
Async XLA Ops:
  0.8 1.6 %copy-start = (bf16[512,2048]{1,0:T(8,128)(2,1)S(1)}, bf16[512,2048]{1,0:T(8,128)(2,1)}, u32[]{:S(2)}) copy-start(bf16[512,2048]{1,0:T(8,128)(2,1)} %orb_hbm.1) | copy-start | bytes 6291460
  2.3 0.7 copy-start.1

commit v4 on v3

--- a/solution.py
+++ b/solution.py
@@ -1,4 +1,5 @@
 import functools
+import math
 
 import jax
 import jax.numpy as jnp
@@ -286,13 +287,13 @@
             (owner, r),
         )
 
-    def turned_copy(owner, place, span, base, b):
+    def turned_copy(owner, span, base, b):
         lo, hi = span
         return remote(
             v_buf.at[b, pl.ds(lo - base, hi - lo)],
-            v_rec.at[place, b, pl.ds(lo - owner * quota, hi - lo)],
+            v_rec.at[b, pl.ds(lo - owner * quota, hi - lo)],
             v_send.at[owner, b],
-            v_recv.at[place, b],
+            v_recv.at[b],
             (owner, source_row),
         )
 
@@ -319,14 +320,14 @@
                             act(beside_copy(owner, a, span, base, b))
 
     def each_turned(b, act):
-        for in_low, base in ((True, 2 * own), (False, 0)):
-
-            @pl.when(jnp.logical_and(has_source, low if in_low else jnp.logical_not(low)))
+        for base, other in ((0, 2 * own), (2 * own, 0)):
+
+            @pl.when(jnp.logical_and(has_source, a == (base + b * piece) // quota))
             def _():
                 for owner in range(aux):
-                    span = part_of(owner, base, 0, own)
+                    span = part_of(owner, other, 0, own)
                     if span is not None:
-                        act(turned_copy(owner, lax.rem(a, half), span, base, b))
+                        act(turned_copy(owner, span, other, b))
 
     def start(copy):
         copy.start()
@@ -405,6 +406,7 @@
                             beside_copy(owner, peer, span, base, c).wait_recv()
                             total += s_rec[peer, lo - first : hi - first]
                     out_ref[lo - first : hi - first] += total
+                    v_buf[c] = total.T.astype(jnp.bfloat16)
 
     def finish_turned(c):
         for owner in range(aux):
@@ -416,11 +418,10 @@
                 def _():
                     lo, hi = span
                     first = owner * quota
-                    for place in range(half):
-                        turned_copy(owner, place, span, base, c).wait_recv()
-                        out_ref[lo - first : hi - first, c * piece : (c + 1) * piece] += v_rec[
-                            place, c, lo - first : hi - first
-                        ].astype(jnp.float32)
+                    turned_copy(owner, span, base, c).wait_recv()
+                    out_ref[lo - first : hi - first, c * piece : (c + 1) * piece] += v_rec[
+                        c, lo - first : hi - first
+                    ].astype(jnp.float32)
 
     out_ref[...] = jnp.zeros_like(out_ref)
     for c in range(chunks):
@@ -431,29 +432,19 @@
             half_copy(0, c).wait_recv()
             half_copy(1, c).wait_recv()
             for other in range(nb):
-                v_buf[c, other * bs : (other + 1) * bs] = product(
-                    [(h2, other, full, rh0, b, inner), (h0, other, full, rh1, b, inner)],
-                    (bs, piece),
-                ).astype(jnp.bfloat16)
-
-        each_turned(c, start)
-
-        @pl.when(has_source)
-        def _():
-            for other in range(nb):
                 w_buf[c, :, other * bs : (other + 1) * bs] = product(
                     [(rh0, b, inner, h2, other, full), (rh1, b, inner, h0, other, full)],
                     (piece, bs),
                 )
 
         each_beside(c, start)
+        finish_beside(c)
+        each_turned(c, start)
         if c == 1:
             finish_diagonal()
         if c >= 1:
-            finish_beside(c - 1)
             finish_turned(c - 1)
 
-    finish_beside(chunks - 1)
     finish_turned(chunks - 1)
 
     for i in range(3):
@@ -486,7 +477,7 @@
     width = occ_count // rows
     scale = 1.0 / (naux * aux * width) ** 0.5
     quota = 3 * own // aux
-    piece = bs // 2
+    piece = math.gcd(bs // 2, quota)
     chunks = own // piece
     if width % 128:
         near = [
@@ -502,10 +493,10 @@
         functools.partial(kernel, aux, rows, scale),
         out_shape=jax.ShapeDtypeStruct((quota, own), jnp.float32),
         in_specs=[
-            pl.BlockSpec(memory_space=pl.ANY),
-            pl.BlockSpec(memory_space=pl.ANY),
-            pl.BlockSpec(memory_space=pl.ANY),
-            pl.BlockSpec(memory_space=pl.ANY),
+            pl.BlockSpec(memory_space=pltpu.HBM),
+            pl.BlockSpec(memory_space=pltpu.HBM),
+            pl.BlockSpec(memory_space=pltpu.HBM),
+            pl.BlockSpec(memory_space=pltpu.HBM),
         ],
         out_specs=pl.BlockSpec(memory_space=pltpu.VMEM),
         scratch_shapes=[
@@ -521,7 +512,7 @@
             pltpu.VMEM((chunks, piece, own), jnp.float32),
             pltpu.VMEM((chunks, own, piece), jnp.bfloat16),
             pltpu.VMEM((aux, quota, own), jnp.float32),
-            pltpu.VMEM((aux // 2, chunks, quota, piece), jnp.bfloat16),
+            pltpu.VMEM((chunks, quota, piece), jnp.bfloat16),
             dma,
             dma((2,)),
             dma((5,)),
@@ -536,7 +527,7 @@
             dma((aux, chunks)),
             dma((aux, chunks)),
             dma((aux, chunks)),
-            dma((aux // 2, chunks)),
+            dma((chunks,)),
         ],
         compiler_params=pltpu.CompilerParams(
             collective_id=0, has_side_effects=True, vmem_limit_bytes=48 * 1024 * 1024

time: 86.4 us -> 80.1 us (0.927)
  Pallas kernels: 82.1 us -> 75.7 us
    pallas_call x1, Pallas kernels: 82.1 us -> 75.7 us  [on_device(): pl.pallas_call(functools.partial(kernel, aux, rows, scale), out_shape=jax...]
where the time goes in v4:
time: 80.1 us; the launch traced here: 79.9 us
  Pallas kernels  75.7 us (95%)
  local copies, waits for them, and re-layouts  4.18 us (5%)
    pallas_call x1, Pallas kernels, on_device(): pl.pallas_call(functools.partial(kernel, aux, rows, scale), out_shape=jax...  75.7 us
    unnamed x5, local copies, waits for them, and re-layouts  3.03 us

profile of v4, /device:TPU:13, one launch (start us, length us, event | category | flops | bytes accessed | tf_op | source)
XLA Modules:
  0.0 79.9 jit_solution(13658463688550820719)
XLA Ops:
  0.0 0.8 copy.5.mask_hbm
  0.8 0.0 copy-start
  0.8 1.6 %copy-done = bf16[512,2048]{1,0:T(8,128)(2,1)S(1)} copy-done((bf16[512,2048]{1,0:T(8,128)(2,1)S(1)}, bf16[512,2048]{1,0:T(8,128)(2,1)}, u32[]{:S(2)}) %copy-start) | copy-done | bytes 2097176
  2.3 0.0 copy-start.1
  2.4 0.7 copy-done.1
  3.0 75.7 %shard_map.46 = f32[384,512]{1,0:T(8,128)S(1)} custom-call(s32[2,4]{1,0:T(2,128)S(1)} %copy-done.1, s32[16,8]{1,0:T(8,128)S(1)} %copy.5.mask_hbm, bf16[512,2048]{1,0:T(8,128)(2,1)S(1)} %copy-done, bf16[4,2,4,256,256]{4,3,2,1,0:T(8,128)(2,1)} %int_hbm.1), custom_call_target="tpu_custom_call" | custom-call | flops 6979321856 | bytes 4194304 | tf_op jit(solution)/shard_map/pallas_call | solution.py:492
  78.7 1.1 %copy.6 = f32[512,384]{1,0:T(8,128)} copy(f32[512,384]{0,1:T(8,128)S(1)} %bitcast.1) | data formatting | bytes 1572864 | tf_op jit(solution)/shard_map/transpose | solution.py:539
Async XLA Ops:
  0.8 1.6 %copy-start = (bf16[512,2048]{1,0:T(8,128)(2,1)S(1)}, bf16[512,2048]{1,0:T(8,128)(2,1)}, u32[]{:S(2)}) copy-start(bf16[512,2048]{1,0:T(8,128)(2,1)} %orb_hbm.1) | copy-start | bytes 6291460
  2.3 0.7 copy-start.1

commit v5 on v4

--- a/solution.py
+++ b/solution.py
@@ -220,7 +220,7 @@
     def transform_slot(i, slot, b):
         at = r - 1 + slot
         inside = jnp.logical_and(at >= 0, at < rows)
-        held_here = mask_ref[r * nb + b, jnp.clip(at, 0, rows - 1)]
+        held_here = mask_ref[jnp.clip(at, 0, rows - 1), r * nb + b]
         factor = jnp.where(inside, held_here, 0).astype(jnp.float32)
         columns = [jnp.clip(cols_ref[b, k] - (r - 1) * nb, 0, 3 * nb - 1) for k in range(kept)]
 
@@ -335,9 +335,11 @@
     def wait_send(copy):
         copy.wait_send()
 
-    for copy in near:
-        copy.wait()
+    for t in (1, 3, 2):
+        near[t].wait()
     send_orbitals(1)
+    for t in (0, 4):
+        near[t].wait()
     share_orbitals(1)
     for slot in (0, 2):
         send_orbitals(slot)
@@ -501,7 +503,7 @@
         out_specs=pl.BlockSpec(memory_space=pltpu.VMEM),
         scratch_shapes=[
             pltpu.SMEM(block_columns.shape, jnp.int32),
-            pltpu.SMEM(occ_mask.shape, jnp.int32),
+            pltpu.SMEM(occ_mask.shape[::-1], jnp.int32),
             pltpu.VMEM(integrals.shape, jnp.bfloat16),
             pltpu.VMEM((5, own, width), jnp.bfloat16),
         ]
@@ -530,12 +532,12 @@
             dma((chunks,)),
         ],
         compiler_params=pltpu.CompilerParams(
-            collective_id=0, has_side_effects=True, vmem_limit_bytes=48 * 1024 * 1024
+            collective_id=0, has_side_effects=True, vmem_limit_bytes=125 * 512 * 1024
         ),
         cost_estimate=pl.CostEstimate(
             flops=flops, bytes_accessed=2 * integrals.size, transcendentals=0
         ),
-    )(block_columns, occ_mask, orbitals, integrals)
+    )(block_columns, occ_mask.T, orbitals, integrals)
     return turned.T
 
 

time: 80.1 us -> 78.8 us (0.984)
  local copies, waits for them, and re-layouts: 4.18 us -> 2.28 us
    unnamed x5 -> x0, local copies, waits for them, and re-layouts: 3.03 us -> none
    transpose x1, local copies, waits for them, and re-layouts: 1.15 us -> 2.28 us  [on_device(): return turned.T]
where the time goes in v5:
time: 78.8 us; the launch traced here: 78.7 us
  Pallas kernels  76.4 us (97%)
  local copies, waits for them, and re-layouts  2.28 us (3%)
    pallas_call x1, Pallas kernels, on_device(): pl.pallas_call(functools.partial(kernel, aux, rows, scale), out_shape=jax...  76.4 us
    transpose x1, local copies, waits for them, and re-layouts, on_device(): return turned.T  2.28 us

profile of v5, /device:TPU:13, one launch (start us, length us, event | category | flops | bytes accessed | tf_op | source)
XLA Modules:
  0.0 78.7 jit_solution(11907397301962343788)
XLA Ops:
  0.0 76.4 %shard_map.46 = f32[384,512]{1,0:T(8,128)} custom-call(s32[2,4]{1,0:T(2,128)} %cols_hbm.1, s32[8,16]{1,0:T(8,128)} %bitcast.3, bf16[512,2048]{1,0:T(8,128)(2,1)} %orb_hbm.1, bf16[4,2,4,256,256]{4,3,2,1,0:T(8,128)(2,1)} %int_hbm.1), custom_call_target="tpu_custom_call" | custom-call | flops 6979321856 | bytes 4194304 | tf_op jit(solution)/shard_map/pallas_call | solution.py:494
  76.4 2.3 %copy.5 = f32[512,384]{1,0:T(8,128)} copy(f32[512,384]{0,1:T(8,128)} %bitcast.2) | data formatting | bytes 1572864 | tf_op jit(solution)/shard_map/transpose | solution.py:541
